TPU v7x, 32 devices: a whole 2x2x4 slice. The times are simulated.
32 devices in a mesh: fsdp: 32 (over z, y, x, core).
Axes of the slice: x: 2, y: 2, z: 4, core: 2. Of those that a mesh axis runs over, the one named last changes fastest.
Arguments:
- tokens: bfloat16 [8192, 1536], P('fsdp'), may hold values from -6 to 6
- norm1_gain: bfloat16 [1536], P('fsdp'), may hold values from 0.5 to 1.5
- w_query: bfloat16 [1536, 1536], P('fsdp'), may hold values from -0.15625 to 0.15625
- w_key: bfloat16 [1536, 768], P('fsdp'), may hold values from -0.15625 to 0.15625
- w_value: bfloat16 [1536, 768], P('fsdp'), may hold values from -0.15625 to 0.15625
- w_out: bfloat16 [1536, 1536], P('fsdp'), may hold values from -1.25 to 1.25
- norm2_gain: bfloat16 [1536], P('fsdp'), may hold values from 0.5 to 1.5
- w_gate: bfloat16 [1536, 4096], P('fsdp'), may hold values from -0.15625 to 0.15625
- w_up: bfloat16 [1536, 4096], P('fsdp'), may hold values from -0.15625 to 0.15625
- w_down: bfloat16 [4096, 1536], P('fsdp'), may hold values from -0.09375 to 0.09375
- cotangent: bfloat16 [8192, 1536], P('fsdp'), may hold values from -6 to 6
Outputs:
- output: bfloat16 [8192, 1536], P('fsdp')
- grad_tokens: float32 [8192, 1536], P('fsdp')
- grad_norm1_gain: float32 [1536], P('fsdp')
- grad_w_query: float32 [1536, 1536], P('fsdp')
- grad_w_key: float32 [1536, 768], P('fsdp')
- grad_w_value: float32 [1536, 768], P('fsdp')
- grad_w_out: float32 [1536, 1536], P('fsdp')
- grad_norm2_gain: float32 [1536], P('fsdp')
- grad_w_gate: float32 [1536, 4096], P('fsdp')
- grad_w_up: float32 [1536, 4096], P('fsdp')
- grad_w_down: float32 [4096, 1536], P('fsdp')
All inputs are finite; a program needn't handle non-finite values.
Results may differ from a plain program's by a relative error of at most 0.015.
Values may be sent and summed in bfloat16 or wider, within the bound.
A program may use at most 384 MiB of HBM per device.

v0:
```python
import jax
import jax.numpy as jnp
from jax import lax
from jax.sharding import PartitionSpec as P

HEADS = 16
KV_HEADS = 8
HEAD_DIM = 96


EPSILON = 1e-05
THETA = 100000.0


def rotary_tables(length, width):
    half = width // 2
    position = jnp.arange(length, dtype=jnp.float32)
    inverse = THETA ** (-(jnp.arange(half, dtype=jnp.float32) * 2.0) / width)
    angles = position[:, None] * inverse[None, :]
    return (jnp.cos(angles)[:, None, :], jnp.sin(angles)[:, None, :])


def rotate(values, cosine, sine):
    half = values.shape[-1] // 2
    first = values[..., :half]
    second = values[..., half:]
    return jnp.concatenate(
        [first * cosine - second * sine, second * cosine + first * sine], axis=-1
    )


def rotate_back(grads, cosine, sine):
    half = grads.shape[-1] // 2
    first = grads[..., :half]
    second = grads[..., half:]
    return jnp.concatenate(
        [first * cosine + second * sine, second * cosine - first * sine], axis=-1
    )


def matmul(left, right):
    return jnp.dot(left, right, preferred_element_type=jnp.float32)


def rows_inner(left, right):
    return lax.dot_general(
        left, right, (((0,), (0,)), ((), ())), preferred_element_type=jnp.float32
    )


def times_transposed(left, right):
    return lax.dot_general(
        left, right, (((1,), (1,)), ((), ())), preferred_element_type=jnp.float32
    )


def by_owner(grad, devices):
    return grad.reshape((devices, grad.shape[0] // devices) + grad.shape[1:])


def owner_totals(received):
    return tuple((jnp.sum(piece, axis=0) for piece in received))


def rms_forward(values, gain):
    inverse = lax.rsqrt(jnp.mean(values * values, axis=-1, keepdims=True) + EPSILON)
    normed = values * inverse
    return (normed, inverse, (normed * gain.astype(jnp.float32)).astype(jnp.bfloat16))


def rms_backward(grad_in, normed, inverse, gain):
    scaled = grad_in * gain.astype(jnp.float32)
    gain_grad = jnp.sum(grad_in * normed, axis=0)
    input_grad = inverse * (scaled - normed * jnp.mean(scaled * normed, axis=-1, keepdims=True))
    return (input_grad, gain_grad)


def block_scores(query_rot, key_rot, start, stop, scale):
    block = stop - start
    scores = (
        jnp.einsum("qkrd,tkd->krqt", query_rot, key_rot, preferred_element_type=jnp.float32) * scale
    )
    allowed = jnp.arange(stop)[None, :] <= (start + jnp.arange(block))[:, None]
    return jnp.where(allowed, scores, -1e30)


def body(
    tokens, norm1_gain, w_query, w_key, w_value, w_out, norm2_gain, w_gate, w_up, w_down, cotangent
):
    length = tokens.shape[0]
    per_group = HEADS // KV_HEADS
    scale = HEAD_DIM ** (-0.5)
    cosine, sine = rotary_tables(length, HEAD_DIM)
    devices = lax.axis_size("fsdp")
    attn_full = (
        lax.all_gather(norm1_gain, "fsdp", axis=0, tiled=True),
        lax.all_gather(w_query, "fsdp", axis=0, tiled=True),
        lax.all_gather(w_key, "fsdp", axis=0, tiled=True),
        lax.all_gather(w_value, "fsdp", axis=0, tiled=True),
        lax.all_gather(w_out, "fsdp", axis=0, tiled=True),
    )
    gain_one, query_weight, key_weight, value_weight, out_weight = attn_full
    inputs = tokens.astype(jnp.float32)
    normed_one, inv_one, act_one = rms_forward(inputs, gain_one)
    query_raw = matmul(act_one, query_weight).reshape(length, HEADS, HEAD_DIM)
    key_raw = matmul(act_one, key_weight).reshape(length, KV_HEADS, HEAD_DIM)
    value_low = (
        matmul(act_one, value_weight).astype(jnp.bfloat16).reshape(length, KV_HEADS, HEAD_DIM)
    )
    query_rot = (
        rotate(query_raw, cosine, sine)
        .astype(jnp.bfloat16)
        .reshape(length, KV_HEADS, per_group, HEAD_DIM)
    )
    key_rot = rotate(key_raw, cosine, sine).astype(jnp.bfloat16)
    index = 0
    start = index * length
    stop = start + length
    scores = block_scores(query_rot, key_rot, start, stop, scale)
    peak = jnp.max(scores, axis=-1, keepdims=True)
    expo = jnp.exp(scores - peak)
    total = jnp.sum(expo, axis=-1, keepdims=True)
    probs = (expo / total).astype(jnp.bfloat16)
    lse_list = [peak + jnp.log(total)]
    outputs_list = jnp.einsum(
        "krqt,tkd->qkrd", probs, value_low, preferred_element_type=jnp.float32
    )
    attended = outputs_list.reshape(length, HEADS * HEAD_DIM).astype(jnp.bfloat16)
    mixed = inputs + matmul(attended, out_weight)
    mlp_full = (
        lax.all_gather(norm2_gain, "fsdp", axis=0, tiled=True),
        lax.all_gather(w_gate, "fsdp", axis=0, tiled=True),
        lax.all_gather(w_up, "fsdp", axis=0, tiled=True),
        lax.all_gather(w_down, "fsdp", axis=0, tiled=True),
    )
    gain_two, gate_weight, up_weight, down_weight = mlp_full
    normed_two, inv_two, act_two = rms_forward(mixed, gain_two)
    gate_val = matmul(act_two, gate_weight)
    up_val = matmul(act_two, up_weight)
    sigma = jax.nn.sigmoid(gate_val)
    silu_val = gate_val * sigma
    hidden = (silu_val * up_val).astype(jnp.bfloat16)
    output = (mixed + matmul(hidden, down_weight)).astype(jnp.bfloat16)
    gain_two, gate_weight, up_weight, down_weight = (
        lax.all_gather(norm2_gain, "fsdp", axis=0, tiled=True),
        lax.all_gather(w_gate, "fsdp", axis=0, tiled=True),
        lax.all_gather(w_up, "fsdp", axis=0, tiled=True),
        lax.all_gather(w_down, "fsdp", axis=0, tiled=True),
    )
    grad_out = cotangent.astype(jnp.float32)
    hidden_grad = times_transposed(cotangent, down_weight)
    gate_grad_b = (hidden_grad * up_val * sigma * (1.0 + gate_val * (1.0 - sigma))).astype(
        jnp.bfloat16
    )
    up_grad_b = (hidden_grad * silu_val).astype(jnp.bfloat16)
    gate_grad = rows_inner(act_two, gate_grad_b)
    up_grad = rows_inner(act_two, up_grad_b)
    act_two_grad = times_transposed(gate_grad_b, gate_weight) + times_transposed(
        up_grad_b, up_weight
    )
    mixed_part, gain_two_grad = rms_backward(act_two_grad, normed_two, inv_two, gain_two)
    mixed_grad = grad_out + mixed_part
    down_grad = rows_inner(hidden, cotangent)
    received = (
        lax.all_to_all(
            by_owner(gain_two_grad, devices).astype(jnp.bfloat16),
            "fsdp",
            split_axis=0,
            concat_axis=0,
            tiled=True,
        ).astype(jnp.float32),
        lax.all_to_all(
            by_owner(gate_grad, devices).astype(jnp.bfloat16),
            "fsdp",
            split_axis=0,
            concat_axis=0,
            tiled=True,
        ).astype(jnp.float32),
        lax.all_to_all(
            by_owner(up_grad, devices).astype(jnp.bfloat16),
            "fsdp",
            split_axis=0,
            concat_axis=0,
            tiled=True,
        ).astype(jnp.float32),
        lax.all_to_all(
            by_owner(down_grad, devices).astype(jnp.bfloat16),
            "fsdp",
            split_axis=0,
            concat_axis=0,
            tiled=True,
        ).astype(jnp.float32),
    )
    mlp_shards = owner_totals(received)
    gain_one, query_weight, key_weight, value_weight, out_weight = (
        lax.all_gather(norm1_gain, "fsdp", axis=0, tiled=True),
        lax.all_gather(w_query, "fsdp", axis=0, tiled=True),
        lax.all_gather(w_key, "fsdp", axis=0, tiled=True),
        lax.all_gather(w_value, "fsdp", axis=0, tiled=True),
        lax.all_gather(w_out, "fsdp", axis=0, tiled=True),
    )
    branch_grad = mixed_grad.astype(jnp.bfloat16)
    attended_grad = (
        times_transposed(branch_grad, out_weight)
        .astype(jnp.bfloat16)
        .reshape(length, KV_HEADS, per_group, HEAD_DIM)
    )
    index = 0
    start = index * length
    stop = start + length
    scores = block_scores(query_rot, key_rot, start, stop, scale)
    probs = jnp.exp(scores - lse_list[index])
    probs_low = probs.astype(jnp.bfloat16)
    prob_grad = jnp.einsum(
        "qkrd,tkd->krqt", attended_grad, value_low, preferred_element_type=jnp.float32
    )
    center = jnp.sum(probs * prob_grad, axis=-1, keepdims=True)
    score_grad = (probs * (prob_grad - center)).astype(jnp.bfloat16)
    query_grads = (
        jnp.einsum("krqt,tkd->qkrd", score_grad, key_rot, preferred_element_type=jnp.float32)
        * scale
    )
    key_term = (
        jnp.einsum("krqt,qkrd->tkd", score_grad, query_rot, preferred_element_type=jnp.float32)
        * scale
    )
    value_term = jnp.einsum(
        "krqt,qkrd->tkd", probs_low, attended_grad, preferred_element_type=jnp.float32
    )
    query_rot_grad = query_grads.reshape(length, HEADS, HEAD_DIM)
    query_raw_grad = (
        rotate_back(query_rot_grad, cosine, sine)
        .astype(jnp.bfloat16)
        .reshape(length, HEADS * HEAD_DIM)
    )
    key_raw_grad = (
        rotate_back(key_term, cosine, sine)
        .astype(jnp.bfloat16)
        .reshape(length, KV_HEADS * HEAD_DIM)
    )
    value_raw_grad = value_term.astype(jnp.bfloat16).reshape(length, KV_HEADS * HEAD_DIM)
    query_wgrad = rows_inner(act_one, query_raw_grad)
    key_wgrad = rows_inner(act_one, key_raw_grad)
    value_wgrad = rows_inner(act_one, value_raw_grad)
    act_one_grad = (
        times_transposed(query_raw_grad, query_weight)
        + times_transposed(key_raw_grad, key_weight)
        + times_transposed(value_raw_grad, value_weight)
    )
    input_part, gain_one_grad = rms_backward(act_one_grad, normed_one, inv_one, gain_one)
    grad_tokens = mixed_grad + input_part
    out_grad = rows_inner(attended, branch_grad)
    received = (
        lax.all_to_all(
            by_owner(gain_one_grad, devices).astype(jnp.bfloat16),
            "fsdp",
            split_axis=0,
            concat_axis=0,
            tiled=True,
        ).astype(jnp.float32),
        lax.all_to_all(
            by_owner(query_wgrad, devices).astype(jnp.bfloat16),
            "fsdp",
            split_axis=0,
            concat_axis=0,
            tiled=True,
        ).astype(jnp.float32),
        lax.all_to_all(
            by_owner(key_wgrad, devices).astype(jnp.bfloat16),
            "fsdp",
            split_axis=0,
            concat_axis=0,
            tiled=True,
        ).astype(jnp.float32),
        lax.all_to_all(
            by_owner(value_wgrad, devices).astype(jnp.bfloat16),
            "fsdp",
            split_axis=0,
            concat_axis=0,
            tiled=True,
        ).astype(jnp.float32),
        lax.all_to_all(
            by_owner(out_grad, devices).astype(jnp.bfloat16),
            "fsdp",
            split_axis=0,
            concat_axis=0,
            tiled=True,
        ).astype(jnp.float32),
    )
    attn_shards = owner_totals(received)
    return (
        output,
        grad_tokens,
        attn_shards[0],
        attn_shards[1],
        attn_shards[2],
        attn_shards[3],
        attn_shards[4],
        mlp_shards[0],
        mlp_shards[1],
        mlp_shards[2],
        mlp_shards[3],
    )


def solution(mesh):
    in_specs = (
        P("fsdp", None),
        P("fsdp"),
        P("fsdp", None),
        P("fsdp", None),
        P("fsdp", None),
        P("fsdp", None),
        P("fsdp"),
        P("fsdp", None),
        P("fsdp", None),
        P("fsdp", None),
        P("fsdp", None),
    )
    out_specs = (
        P("fsdp", None),
        P("fsdp", None),
        P("fsdp"),
        P("fsdp", None),
        P("fsdp", None),
        P("fsdp", None),
        P("fsdp", None),
        P("fsdp"),
        P("fsdp", None),
        P("fsdp", None),
        P("fsdp", None),
    )
    return jax.shard_map(body, mesh=mesh, in_specs=in_specs, out_specs=out_specs, check_vma=False)
```

profile of v0, /device:TPU:0, one launch (start us, length us, event | category | flops | bytes accessed | tf_op | source)
XLA Modules:
  0.0 1825.5 jit_solution(1132701463898646250)
XLA Ops:
  13.6 42.2 %all-reduce.2 = (bf16[1536]{0:T(1024)(128)(2,1)S(1)}, bf16[1536]{0:T(1024)(128)(2,1)S(1)}) all-reduce(bf16[1536]{0:T(1024)(128)(2,1)S(1)} %dynamic-update-slice, bf16[1536]{0:T(1024)(128)(2,1)S(1)} %dynamic-update-slice.1), channel_id=1, replica_groups=mesh['fsdp'=32] {'fsdp'}, use_global_device_ids=true, to_apply=%add | all-reduce | flops 3072 | bytes 12288
  58.2 12.8 all-gather.8.cloned.1.call-done
  73.6 56.4 %all-gather.10.cloned.1.call-done = bf16[1536,768]{1,0:T(8,128)(2,1)} async-done(((bf16[48,768]{1,0:T(8,128)(2,1)}), bf16[1536,768]{1,0:T(8,128)(2,1)}) %all-gather.10.cloned.1.call-update) | async-done | bytes 2359312 | tf_op jit(solution)/shard_map/all_gather | solution.py:98
  133.0 62.6 %all-gather.12.cloned.1.call-done = bf16[1536,1536]{1,0:T(8,128)(2,1)} async-done(((bf16[48,1536]{1,0:T(8,128)(2,1)}), bf16[1536,1536]{1,0:T(8,128)(2,1)}) %all-gather.12.cloned.1.call-update) | async-done | bytes 4718608 | tf_op jit(solution)/shard_map/all_gather | solution.py:97
  203.9 56.8 %all-gather.14.cloned.1.call-done = bf16[1536,1536]{1,0:T(8,128)(2,1)} async-done(((bf16[48,1536]{1,0:T(8,128)(2,1)}), bf16[1536,1536]{1,0:T(8,128)(2,1)}) %all-gather.14.cloned.1.call-update) | async-done | bytes 4718608 | tf_op jit(solution)/shard_map/all_gather | solution.py:100
  264.9 93.4 %all-gather.18.cloned.1.call-done = bf16[1536,4096]{1,0:T(8,128)(2,1)} async-done(((bf16[48,4096]{1,0:T(8,128)(2,1)}), bf16[1536,4096]{1,0:T(8,128)(2,1)}) %all-gather.18.cloned.1.call-update) | async-done | bytes 12582928 | tf_op jit(solution)/shard_map/all_gather | solution.py:133
  358.3 9.5 fusion.47
  367.8 87.5 %all-gather.16.cloned.1.call-done = bf16[1536,4096]{1,0:T(8,128)(2,1)} async-done(((bf16[48,4096]{1,0:T(8,128)(2,1)}), bf16[1536,4096]{1,0:T(8,128)(2,1)}) %all-gather.16.cloned.1.call-update) | async-done | bytes 12582928 | tf_op jit(solution)/shard_map/all_gather | solution.py:132
  455.3 9.7 fusion.46
  464.9 87.4 %all-gather.20.cloned.1.call-done = bf16[4096,1536]{1,0:T(8,128)(2,1)} async-done(((bf16[128,1536]{1,0:T(8,128)(2,1)}), bf16[4096,1536]{1,0:T(8,128)(2,1)}) %all-gather.20.cloned.1.call-update) | async-done | bytes 12582928 | tf_op jit(solution)/shard_map/all_gather | solution.py:134
  552.4 10.7 multiply_convert_fusion
  570.5 8.5 multiply_reduce_fusion
  633.0 51.3 %all-to-all-done.3 = bf16[32,48,768]{2,1,0:T(8,128)(2,1)} async-done(((bf16[32,48,768]{2,1,0:T(8,128)(2,1)}), bf16[32,48,768]{2,1,0:T(8,128)(2,1)}, u32[]{:S(2)}, u32[]{:S(2)}) %all-to-all-start.3) | async-done | bytes 2359328 | tf_op jit(solution)/shard_map/all_to_all | solution.py:275
  693.2 49.8 %all-to-all-done.2 = bf16[32,48,768]{2,1,0:T(8,128)(2,1)} async-done(((bf16[32,48,768]{2,1,0:T(8,128)(2,1)}), bf16[32,48,768]{2,1,0:T(8,128)(2,1)}, u32[]{:S(2)}, u32[]{:S(2)}) %all-to-all-start.2) | async-done | bytes 2359328 | tf_op jit(solution)/shard_map/all_to_all | solution.py:268
  752.0 100.4 %all-to-all-done.4 = bf16[32,48,1536]{2,1,0:T(8,128)(2,1)} async-done(((bf16[32,48,1536]{2,1,0:T(8,128)(2,1)}), bf16[32,48,1536]{2,1,0:T(8,128)(2,1)}, u32[]{:S(2)}, u32[]{:S(2)}) %all-to-all-start.4) | async-done | bytes 4718624 | tf_op jit(solution)/shard_map/all_to_all | solution.py:282
  856.3 9.8 convolution_convert_fusion
  866.1 95.5 %all-to-all-done.1 = bf16[32,48,1536]{2,1,0:T(8,128)(2,1)} async-done(((bf16[32,48,1536]{2,1,0:T(8,128)(2,1)}), bf16[32,48,1536]{2,1,0:T(8,128)(2,1)}, u32[]{:S(2)}, u32[]{:S(2)}) %all-to-all-start.1) | async-done | bytes 4718624 | tf_op jit(solution)/shard_map/all_to_all | solution.py:261
  965.5 9.8 convolution_convert_fusion.1
  975.3 268.9 %all-to-all-done.8 = bf16[32,128,1536]{2,1,0:T(8,128)(2,1)} async-done(((bf16[32,128,1536]{2,1,0:T(8,128)(2,1)}), bf16[32,128,1536]{2,1,0:T(8,128)(2,1)}, u32[]{:S(2)}, u32[]{:S(2)}) %all-to-all-start.8) | async-done | bytes 12582944 | tf_op jit(solution)/shard_map/all_to_all | solution.py:186
  1248.1 9.8 convolution_convert_fusion.2
  1257.9 269.1 %all-to-all-done.7 = bf16[32,48,4096]{2,1,0:T(8,128)(2,1)} async-done(((bf16[32,48,4096]{2,1,0:T(8,128)(2,1)}), bf16[32,48,4096]{2,1,0:T(8,128)(2,1)}, u32[]{:S(2)}, u32[]{:S(2)}) %all-to-all-start.7) | async-done | bytes 12582944 | tf_op jit(solution)/shard_map/all_to_all | solution.py:179
  1564.7 8.5 convert_reduce_fusion.1
  1573.3 236.5 %all-to-all-done.6 = bf16[32,48,4096]{2,1,0:T(8,128)(2,1)} async-done(((bf16[32,48,4096]{2,1,0:T(8,128)(2,1)}), bf16[32,48,4096]{2,1,0:T(8,128)(2,1)}, u32[]{:S(2)}, u32[]{:S(2)}) %all-to-all-start.6) | async-done | bytes 12582944 | tf_op jit(solution)/shard_map/all_to_all | solution.py:172
  1809.7 8.5 convert_reduce_fusion.2
  (173 shorter events, 154.8 us)
Async XLA Ops:
  7.2 63.8 %all-gather.8.cloned.1.call-start = ((), (), s32[]{:S(2)}) async-start(), calls=%async_computation.9 | async-start | bytes 2433024 | tf_op jit(solution)/shard_map/all_gather | solution.py:99
  7.9 122.1 %all-gather.10.cloned.1.call-start = ((), (), s32[]{:S(2)}) async-start(), calls=%async_computation.10 | async-start | bytes 2433024 | tf_op jit(solution)/shard_map/all_gather | solution.py:98
  8.7 186.8 %all-gather.12.cloned.1.call-start = ((), (), s32[]{:S(2)}) async-start(), calls=%async_computation.11 | async-start | bytes 4866048 | tf_op jit(solution)/shard_map/all_gather | solution.py:97
  9.4 251.3 %all-gather.14.cloned.1.call-start = ((), (), s32[]{:S(2)}) async-start(), calls=%async_computation.12 | async-start | bytes 4866048 | tf_op jit(solution)/shard_map/all_gather | solution.py:100
  10.0 348.3 %all-gather.18.cloned.1.call-start = ((), (), s32[]{:S(2)}) async-start(), calls=%async_computation.14 | async-start | bytes 12976128 | tf_op jit(solution)/shard_map/all_gather | solution.py:133
  10.6 444.7 %all-gather.16.cloned.1.call-start = ((), (), s32[]{:S(2)}) async-start(), calls=%async_computation.13 | async-start | bytes 12976128 | tf_op jit(solution)/shard_map/all_gather | solution.py:132
  11.1 541.2 %all-gather.20.cloned.1.call-start = ((), (), s32[]{:S(2)}) async-start(), calls=%async_computation.15 | async-start | bytes 12976128 | tf_op jit(solution)/shard_map/all_gather | solution.py:134
  55.8 139.7 %copy-start.28 = (f32[1536]{0:T(1024)}, f32[1536]{0:T(1024)S(1)}, u32[]{:S(2)}) copy-start(f32[1536]{0:T(1024)S(1)} %convert_element_type.182) | copy-start | bytes 18436
  57.9 137.6 %copy-start.36 = (f32[256]{0:T(256)}, f32[256]{0:T(256)S(1)}, u32[]{:S(2)}) copy-start(f32[256]{0:T(256)S(1)} %add_rsqrt_fusion.1) | copy-start | bytes 3076
  58.1 141.7 %copy-start.20 = (f32[256,48]{0,1:T(8,128)}, f32[256,48]{0,1:T(8,128)S(1)}, u32[]{:S(2)}) copy-start(f32[256,48]{0,1:T(8,128)S(1)} %get-tuple-element.29) | copy-start | bytes 147460
  58.1 141.7 %copy-start.22 = (f32[256,48]{0,1:T(8,128)}, f32[256,48]{0,1:T(8,128)S(1)}, u32[]{:S(2)}) copy-start(f32[256,48]{0,1:T(8,128)S(1)} %get-tuple-element.30) | copy-start | bytes 147460
  132.9 67.2 %copy-start.24 = (bf16[256,8,48]{0,2,1:T(8,128)(2,1)}, bf16[256,8,48]{0,2,1:T(8,128)(2,1)S(1)}, u32[]{:S(2)}) copy-start(bf16[256,8,48]{0,2,1:T(8,128)(2,1)S(1)} %get-tuple-element.26) | copy-start | bytes 589828
  264.6 93.6 %copy-start.38 = (f32[256]{0:T(256)}, f32[256]{0:T(256)S(1)}, u32[]{:S(2)}) copy-start(f32[256]{0:T(256)S(1)} %add_rsqrt_fusion) | copy-start | bytes 3076
  264.9 190.4 %copy-start.5 = (bf16[256,1536]{1,0:T(8,128)(2,1)}, bf16[256,1536]{1,0:T(8,128)(2,1)S(1)}, u32[]{:S(2)}) copy-start(bf16[256,1536]{1,0:T(8,128)(2,1)S(1)} %multiply_convert_fusion.3) | copy-start | bytes 2359300
  367.8 184.6 %copy-start.10 = (bf16[256,1536]{1,0:T(8,128)(2,1)S(1)}, bf16[256,1536]{1,0:T(8,128)(2,1)}, u32[]{:S(2)}) copy-start(bf16[256,1536]{1,0:T(8,128)(2,1)} %param.21) | copy-start | bytes 2359300
  594.4 19.0 %all-to-all-start.5 = ((bf16[32,1,48]{2,1,0:T(2,128)(2,1)}), bf16[32,1,48]{2,1,0:T(2,128)(2,1)}, u32[]{:S(2)}, u32[]{:S(2)}) async-start(bf16[32,1,48]{2,1,0:T(2,128)(2,1)} %convert_element_type.230), calls=%async_computation.5 | async-start | bytes 32768 | tf_op jit(solution)/shard_map/all_to_all | solution.py:165
  613.4 12.8 all-to-all-start
  626.2 58.1 %all-to-all-start.3 = ((bf16[32,48,768]{2,1,0:T(8,128)(2,1)}), bf16[32,48,768]{2,1,0:T(8,128)(2,1)}, u32[]{:S(2)}, u32[]{:S(2)}) async-start(bf16[32,48,768]{2,1,0:T(8,128)(2,1)} %convolution_convert_fusion.6), calls=%async_computation.3 | async-start | bytes 4718592 | tf_op jit(solution)/shard_map/all_to_all | solution.py:275
  684.3 58.7 %all-to-all-start.2 = ((bf16[32,48,768]{2,1,0:T(8,128)(2,1)}), bf16[32,48,768]{2,1,0:T(8,128)(2,1)}, u32[]{:S(2)}, u32[]{:S(2)}) async-start(bf16[32,48,768]{2,1,0:T(8,128)(2,1)} %convolution_convert_fusion.7), calls=%async_computation.2 | async-start | bytes 4718592 | tf_op jit(solution)/shard_map/all_to_all | solution.py:268
  743.0 109.4 %all-to-all-start.4 = ((bf16[32,48,1536]{2,1,0:T(8,128)(2,1)}), bf16[32,48,1536]{2,1,0:T(8,128)(2,1)}, u32[]{:S(2)}, u32[]{:S(2)}) async-start(bf16[32,48,1536]{2,1,0:T(8,128)(2,1)} %convolution_convert_fusion.3), calls=%async_computation.4 | async-start | bytes 9437184 | tf_op jit(solution)/shard_map/all_to_all | solution.py:282
  852.4 109.2 %all-to-all-start.1 = ((bf16[32,48,1536]{2,1,0:T(8,128)(2,1)}), bf16[32,48,1536]{2,1,0:T(8,128)(2,1)}, u32[]{:S(2)}, u32[]{:S(2)}) async-start(bf16[32,48,1536]{2,1,0:T(8,128)(2,1)} %convolution_convert_fusion.4), calls=%async_computation.1 | async-start | bytes 9437184 | tf_op jit(solution)/shard_map/all_to_all | solution.py:261
  961.6 282.6 %all-to-all-start.8 = ((bf16[32,128,1536]{2,1,0:T(8,128)(2,1)}), bf16[32,128,1536]{2,1,0:T(8,128)(2,1)}, u32[]{:S(2)}, u32[]{:S(2)}) async-start(bf16[32,128,1536]{2,1,0:T(8,128)(2,1)} %bitcast.119), calls=%async_computation.8 | async-start | bytes 25165824 | tf_op jit(solution)/shard_map/all_to_all | solution.py:186
  1244.2 282.7 %all-to-all-start.7 = ((bf16[32,48,4096]{2,1,0:T(8,128)(2,1)}), bf16[32,48,4096]{2,1,0:T(8,128)(2,1)}, u32[]{:S(2)}, u32[]{:S(2)}) async-start(bf16[32,48,4096]{2,1,0:T(8,128)(2,1)} %bitcast.121), calls=%async_computation.7 | async-start | bytes 25165824 | tf_op jit(solution)/shard_map/all_to_all | solution.py:179
  1526.9 282.8 %all-to-all-start.6 = ((bf16[32,48,4096]{2,1,0:T(8,128)(2,1)}), bf16[32,48,4096]{2,1,0:T(8,128)(2,1)}, u32[]{:S(2)}, u32[]{:S(2)}) async-start(bf16[32,48,4096]{2,1,0:T(8,128)(2,1)} %bitcast.120), calls=%async_computation.6 | async-start | bytes 25165824 | tf_op jit(solution)/shard_map/all_to_all | solution.py:172
  (36 other events, 319.0 us)
Sparse Core Ops, SparseCore 0:
  10.9 60.0 all-gather.7
  73.9 56.1 all-gather.9
  132.9 62.5 all-gather.11
  198.3 62.4 all-gather.13
  263.5 94.7 all-gather.17
  361.0 94.2 all-gather.15
  458.1 94.2 all-gather.19
where the time goes:
time: 1840 us; the launch traced here: 1830 us
  waiting for transfers between devices  1540 us (84%)
  matrix products  131 us (7%)
  other arithmetic  53 us (3%)
  blocking collectives  42.2 us (2%)
  starting transfers between devices  36.6 us (2%)
    all_to_all x1, waiting for transfers between devices, body(): lax.all_to_all(by_owner(up_grad, devices).astype(jnp.bfloat16), 'fsdp', s...  269 us
    all_to_all x1, waiting for transfers between devices, body(): lax.all_to_all(by_owner(down_grad, devices).astype(jnp.bfloat16), 'fsdp',...  269 us
    all_to_all x1, waiting for transfers between devices, body(): lax.all_to_all(by_owner(gate_grad, devices).astype(jnp.bfloat16), 'fsdp',...  236 us
    all_to_all x1, waiting for transfers between devices, body(): lax.all_to_all(by_owner(out_grad, devices).astype(jnp.bfloat16), 'fsdp',...  100 us
    all_to_all x1, waiting for transfers between devices, body(): lax.all_to_all(by_owner(query_wgrad, devices).astype(jnp.bfloat16), 'fsdp...  95.5 us
    all_gather x1, waiting for transfers between devices, body(): lax.all_gather(w_up, 'fsdp', axis=0, tiled=True)  93.4 us
    all_gather x1, waiting for transfers between devices, body(): lax.all_gather(w_gate, 'fsdp', axis=0, tiled=True)  87.5 us
    all_gather x1, waiting for transfers between devices, body(): lax.all_gather(w_down, 'fsdp', axis=0, tiled=True)  87.4 us
  transfers between devices with their start and end apart: 16, of which 15 were waited for; matrix products, arithmetic and copies ran while one was open for 8% of the time, Pallas kernels for 0%

commit v1 on v0

v1 whole, which is shorter than its diff:
```python
import functools
import types

import jax
import jax.numpy as jnp
from jax import lax
from jax.experimental import pallas as pl
from jax.experimental.pallas import tpu as pltpu
from jax.sharding import PartitionSpec as P

HEADS = 16
KV_HEADS = 8
HEAD_DIM = 96
EPSILON = 1e-05
THETA = 100000.0

AXIS = "fsdp"
GROUP = 8
MESH = pl.DeviceIdType.MESH
BF = jnp.bfloat16
F32 = jnp.float32
ANY = pl.BlockSpec(memory_space=pl.ANY)
VM = pl.BlockSpec(memory_space=pltpu.VMEM)
DMA = pltpu.SemaphoreType.DMA


def place():
    me = lax.axis_index(AXIS)
    p, r = lax.rem(me, GROUP), lax.div(me, GROUP)
    c = lax.rem(me, 2)
    x = lax.rem(lax.div(me, 2), 2)
    y = lax.rem(lax.div(me, 4), 2)
    to_x, to_y, to_c = 2 - 4 * x, 4 - 8 * y, 1 - 2 * c
    k0 = y * 2 + x
    kx, ky = k0 + 1 - 2 * x, k0 + 2 - 4 * y
    return types.SimpleNamespace(
        me=me, p=p, r=r, c=c, core=me + to_c, xn=me + to_x, yn=me + to_y,
        up=me + GROUP, dn=me - GROUP, to_c=to_c,
        px=p + to_x, py=p + to_y, pd=p + to_x + to_y,
        k0=k0, kx=kx, ky=ky, kd=kx + ky - k0,
    )


def when(cond, do):
    if cond is None:
        do()
    else:
        pl.when(cond)(do)


def both(a, b):
    if a is None:
        return b
    if b is None:
        return a
    return jnp.logical_and(a, b)


class Book:
    def __init__(self, at):
        self.at, self.sent = at, []

    def send(self, src, dst, ss, rs, dev, cond=None):
        def copy():
            return pltpu.make_async_remote_copy(
                src_ref=src, dst_ref=dst, send_sem=ss, recv_sem=rs,
                device_id=(dev,), device_id_type=MESH,
            )

        when(cond, lambda: copy().start())
        self.sent.append((cond, copy))

    def got(self, dst, rs, cond=None):
        def wait():
            pltpu.make_async_remote_copy(
                src_ref=dst, dst_ref=dst, send_sem=rs, recv_sem=rs,
                device_id=(self.at.core,), device_id_type=MESH,
            ).wait_recv()

        when(cond, wait)

    def drain(self):
        for cond, copy in self.sent:
            when(cond, lambda: copy().wait_send())


def meet(at, groups, plane, line):
    bar = pltpu.get_barrier_semaphore()

    def greet(dev):
        pl.semaphore_signal(bar, inc=1, device_id=(dev,), device_id_type=MESH)

    if plane == "all":
        peers = [at.me - at.p + lax.rem(at.p + k, GROUP) for k in range(1, GROUP)]
    else:
        peers = [at.core, at.xn, at.yn]
    for dev in peers:
        greet(dev)
    count = len(peers)
    if line:
        pl.when(at.r < groups - 1)(lambda: greet(at.up))
        pl.when(at.r > 0)(lambda: greet(at.dn))
        ends = jnp.where(at.r > 0, 1, 0) + jnp.where(at.r < groups - 1, 1, 0)
        count = count + ends
    pl.semaphore_wait(bar, count)


class PlaneGather:
    def __init__(self, at, book, pos, rs, ss):
        self.at, self.book, self.pos, self.rs, self.ss = at, book, pos, rs, ss

    def own(self, i, src, cond=None):
        at, dst, rs = self.at, self.pos(i, self.at.p), self.rs(i, self.at.p)
        self.book.send(src, dst, self.ss(i, 0), rs, at.xn, cond)
        self.book.send(src, dst, self.ss(i, 1), rs, at.yn, cond)
        self.book.send(src, dst, self.ss(i, 2), rs, at.core, cond)

    def event(self, i, odd, cond=None):
        at = self.at
        for q, kind in ((at.px, 3), (at.py, 5), (at.pd, 7)):
            dst, rs = self.pos(i, q), self.rs(i, q)
            self.book.got(dst, rs, cond)
            if kind == 3:
                self.fwd(dst, self.ss(i, 4), rs, at.yn, cond, odd, True)
            if kind == 5:
                self.fwd(dst, self.ss(i, 6), rs, at.xn, cond, odd, False)
            self.book.send(dst, dst, self.ss(i, kind), rs, at.core, cond)

    def fwd(self, dst, ss, rs, dev, cond, odd, on_odd):
        if isinstance(odd, bool):
            if odd == on_odd:
                self.book.send(dst, dst, ss, rs, dev, cond)
        else:
            mine = odd if on_odd else jnp.logical_not(odd)
            self.book.send(dst, dst, ss, rs, dev, both(cond, mine))

    def finish(self, i, cond=None):
        at = self.at
        for q in (at.p, at.px, at.py, at.pd):
            q = q + at.to_c
            self.book.got(self.pos(i, q), self.rs(i, q), cond)


class LineGather:
    def __init__(self, at, book, groups, pos, rs, ss):
        self.at, self.book, self.groups = at, book, groups
        self.pos, self.rs, self.ss = pos, rs, ss

    def own(self, src):
        r, dst = self.at.r, self.pos(self.at.r)
        self.book.send(src, dst, self.ss(r, 0), self.rs(r), self.at.up, r < self.groups - 1)
        self.book.send(src, dst, self.ss(r, 1), self.rs(r), self.at.dn, r > 0)

    def step(self, d, then=None):
        r, last = self.at.r, self.groups - 1
        below, above = r >= d, r + d <= last
        for q, here, go, kind, dev in (
            (r - d, below, r < last, 0, self.at.up),
            (r + d, above, r > 0, 1, self.at.dn),
        ):
            dst = self.pos(q)
            self.book.got(dst, self.rs(q), here)
            self.book.send(dst, dst, self.ss(q, kind), self.rs(q), dev, both(here, go))
            if then is not None:
                then(q, here, dst)


def around(r, d, last):
    if d == 0:
        return [(r, None)]
    return [(r - d, r >= d), (r + d, r + d <= last)]


def gather_kernel(
    R, NE, q_i, o_i, gu_i, wd_i, e_i, q_o, o_o, gu_o, wd_o, e_o,
    lsem, qr, qz, qp, orr, oz, op, gar, gas, gzr, gzs, dr, ds_, er, es,
):
    at = place()
    meet(at, R, "all", True)
    book = Book(at)
    r, last = at.r, R - 1

    def full(inp, out, rs, zs, ps):
        def slot(i, q):
            return i * GROUP + q

        plane = PlaneGather(
            at, book, lambda i, q: out.at[slot(i, q)], lambda i, q: rs.at[slot(i, q)],
            lambda i, k: ps.at[i, k],
        )
        line = LineGather(
            at, book, R, lambda i: out.at[slot(i, at.p)], lambda i: rs.at[slot(i, at.p)],
            lambda i, k: zs.at[i, k],
        )

        def events(d):
            for i, cond in around(r, d, last):
                plane.event(i, lax.rem(i, 2) == 1, cond)

        def finish(d):
            for i, cond in around(r, d, last):
                plane.finish(i, cond)

        return types.SimpleNamespace(
            start=lambda: (line.own(inp), plane.own(r, inp)),
            line=lambda d: line.step(d, lambda i, cond, dst: plane.own(i, dst, cond)),
            events=events, finish=finish,
        )

    q = full(q_i, q_o, qr, qz, qp)
    o = full(o_i, o_o, orr, oz, op)
    q.start()
    o.start()
    mine = [
        pltpu.make_async_copy(q_i, q_o.at[at.me], lsem.at[0]),
        pltpu.make_async_copy(o_i, o_o.at[at.me], lsem.at[1]),
        pltpu.make_async_copy(gu_i.at[at.p], gu_o.at[at.me], lsem.at[2]),
        pltpu.make_async_copy(wd_i, wd_o.at[r], lsem.at[3]),
        pltpu.make_async_copy(e_i, e_o.at[at.p], lsem.at[4]),
    ]
    for copy in mine:
        copy.start()
    for k in range(1, GROUP):
        t = lax.rem(at.p + k, GROUP)
        book.send(gu_i.at[t], gu_o.at[at.me], gas.at[k - 1], gar.at[k - 1], at.me - at.p + t)

    gu_line = LineGather(
        at, book, R, lambda i: gu_o.at[pl.ds(i * GROUP, GROUP)], lambda i: gzr.at[i],
        lambda i, k: gzs.at[i, k],
    )
    wd_line = LineGather(
        at, book, R, lambda i: wd_o.at[i], lambda i: dr.at[i], lambda i, k: ds_.at[i, k]
    )

    for d in range(1, R):
        q.line(d)
        o.line(d)
        q.events(d - 1)
        if d == max(1, R - 2):
            for k in range(1, GROUP):
                t = lax.rem(at.p + GROUP - k, GROUP)
                book.got(gu_o.at[r * GROUP + t], gar.at[k - 1])
            for copy in mine:
                copy.wait()
    gu_line.own(gu_o.at[pl.ds(r * GROUP, GROUP)])
    wd_line.own(wd_i)
    q.events(R - 1)
    o.events(0)
    for d in range(1, R):
        if d == 2:
            e_events = e_start(at, book, NE, e_i, e_o, er, es)
        gu_line.step(d)
        o.events(d)
        wd_line.step(d)
        if d == R - 2:
            e_events()
    for d in range(R):
        q.finish(d)
        o.finish(d)
    e_events(True)
    book.drain()


def e_start(at, book, parts, e_i, e_o, er, es):
    rows = e_i.shape[0] // parts

    def part(i):
        return pl.ds(i * rows, rows)

    plane = PlaneGather(
        at, book, lambda i, q: e_o.at[q, part(i)], lambda i, q: er.at[i, q],
        lambda i, k: es.at[i, k],
    )
    for i in range(parts):
        plane.own(i, e_i.at[part(i)])

    def events(finish=False):
        for i in range(parts):
            if finish:
                plane.finish(i)
            else:
                plane.event(i, i % 2 == 1)

    return events


def gather_weights(R, q, o, gu, wd, e):
    n = R * GROUP
    rows, parts = q.shape[0], 4
    return pl.pallas_call(
        functools.partial(gather_kernel, R, parts),
        out_shape=(
            jax.ShapeDtypeStruct((n, rows, q.shape[1]), BF),
            jax.ShapeDtypeStruct((n, rows, o.shape[1]), BF),
            jax.ShapeDtypeStruct((n, rows, gu.shape[2]), BF),
            jax.ShapeDtypeStruct((R,) + wd.shape, BF),
            jax.ShapeDtypeStruct((GROUP,) + e.shape, BF),
        ),
        in_specs=[ANY] * 5,
        out_specs=(ANY,) * 5,
        scratch_shapes=[
            DMA((5,)),
            DMA((n,)), DMA((R, 2)), DMA((R, 8)),
            DMA((n,)), DMA((R, 2)), DMA((R, 8)),
            DMA((7,)), DMA((7,)), DMA((R,)), DMA((R, 2)),
            DMA((R,)), DMA((R, 2)),
            DMA((parts, GROUP)), DMA((parts, 8)),
        ],
        compiler_params=pltpu.CompilerParams(collective_id=0, has_side_effects=True),
    )(q, o, gu, wd, e)


def spread_kernel(parts, a_i, a_o, lsem, er, es):
    at = place()
    meet(at, 1, "near", False)
    book = Book(at)
    own = pltpu.make_async_copy(a_i, a_o.at[at.p], lsem)
    own.start()
    events = e_start(at, book, parts, a_i, a_o, er, es)
    events()
    events(True)
    own.wait()
    book.drain()


def spread(a):
    parts = 4
    return pl.pallas_call(
        functools.partial(spread_kernel, parts),
        out_shape=jax.ShapeDtypeStruct((GROUP,) + a.shape, a.dtype),
        in_specs=[ANY],
        out_specs=ANY,
        scratch_shapes=[DMA, DMA((parts, GROUP)), DMA((parts, 8))],
        compiler_params=pltpu.CompilerParams(collective_id=1, has_side_effects=True),
    )(a)


def add_rows(out, terms):
    step = 16

    def body(i, carry):
        at = pl.ds(pl.multiple_of(i * step, step), step)
        total = terms[0][at, :].astype(F32)
        for term in terms[1:]:
            total = total + term[at, :].astype(F32)
        out[at, :] = total.astype(out.dtype)
        return carry

    lax.fori_loop(0, out.shape[0] // step, body, 0)


class PlaneSum:
    def __init__(self, at, book, odd, pairs, mine, other, diag, from_x, from_y, sem):
        self.at, self.book, self.odd, self.pairs = at, book, odd, pairs
        self.mine, self.other, self.diag = mine, other, diag
        self.from_x, self.from_y, self.sem = from_x, from_y, sem

    def loads(self):
        c = self.at.c
        return [
            pltpu.make_async_copy(src(c), dst(self.mine), self.sem(j))
            for j, (src, dst) in enumerate(self.pairs)
        ]

    def start(self):
        for load in self.loads():
            load.start()
        for j, (src, dst) in enumerate(self.pairs):
            self.book.send(
                src(1 - self.at.c), dst(self.other), self.sem(2 + j), self.sem(4 + j), self.at.core
            )

    def fold(self, k):
        add_rows(self.mine.at[k], [self.mine.at[k], self.other.at[k]])

    def first(self):
        at, book = self.at, self.book
        for load in self.loads():
            load.wait()
        for j, (src, dst) in enumerate(self.pairs):
            book.got(dst(self.other), self.sem(4 + j))
        dev = at.yn if self.odd else at.xn
        self.fold(at.kd)
        book.send(self.mine.at[at.kd], self.diag, self.sem(6), self.sem(7), dev)
        if self.odd:
            self.fold(at.ky)
            book.send(self.mine.at[at.ky], self.from_y, self.sem(8), self.sem(9), at.yn)
            self.fold(at.kx)
        else:
            self.fold(at.kx)
            book.send(self.mine.at[at.kx], self.from_x, self.sem(8), self.sem(9), at.xn)
            self.fold(at.ky)
        self.fold(at.k0)

    def second(self):
        at, book = self.at, self.book
        book.got(self.diag, self.sem(7))
        k = at.kx if self.odd else at.ky
        add_rows(self.mine.at[k], [self.mine.at[k], self.diag])
        if self.odd:
            book.send(self.mine.at[at.kx], self.from_x, self.sem(10), self.sem(11), at.xn)
        else:
            book.send(self.mine.at[at.ky], self.from_y, self.sem(10), self.sem(11), at.yn)

    def third(self, out):
        at, book = self.at, self.book
        book.got(self.from_x, self.sem(11 if self.odd else 9))
        book.got(self.from_y, self.sem(9 if self.odd else 11))
        add_rows(out, [self.mine.at[at.k0], self.from_x, self.from_y])


def row_items(at, book, src, parts, mine, other, diag, from_x, from_y, sems):
    rows = src.shape[2] // parts
    items = []
    for i in range(parts):
        cut = pl.ds(i * rows, rows)
        items.append(
            PlaneSum(
                at, book, i % 2 == 1,
                [(lambda c, cut=cut: src.at[:, c, cut], lambda buf: buf)],
                mine.at[i], other.at[i], diag.at[i], from_x.at[i], from_y.at[i],
                lambda j, i=i: sems.at[i, j],
            )
        )
    return items


def row_scratch(parts, rows, columns):
    rows = rows // parts
    return [
        pltpu.VMEM((parts, 4, rows, columns), BF),
        pltpu.VMEM((parts, 4, rows, columns), BF),
        pltpu.VMEM((parts, rows, columns), BF),
        pltpu.VMEM((parts, rows, columns), BF),
        pltpu.VMEM((parts, rows, columns), BF),
        DMA((parts, 12)),
    ]


def fold_kernel(parts, a_i, a_o, mine, other, diag, from_x, from_y, sems):
    at = place()
    meet(at, 1, "near", False)
    book = Book(at)
    items = row_items(at, book, a_i, parts, mine, other, diag, from_x, from_y, sems)
    rows = a_o.shape[0] // parts
    for item in items:
        item.start()
    for i in range(parts + 2):
        if i < parts:
            items[i].first()
        if 1 <= i <= parts:
            items[i - 1].second()
        if i >= 2:
            items[i - 2].third(a_o.at[pl.ds((i - 2) * rows, rows)])
    book.drain()


def fold(a):
    parts = 4
    rows, columns = a.shape[2:]
    return pl.pallas_call(
        functools.partial(fold_kernel, parts),
        out_shape=jax.ShapeDtypeStruct((rows, columns), F32),
        in_specs=[ANY],
        out_specs=VM,
        scratch_shapes=row_scratch(parts, rows, columns),
        compiler_params=pltpu.CompilerParams(
            collective_id=2, has_side_effects=True, vmem_limit_bytes=50 * 2**20
        ),
    )(a)


class LineSum:
    def __init__(self, at, book, groups, whole, part, inbox, views, rs, ss):
        self.at, self.book, self.groups, self.whole = at, book, groups, whole
        self.part, self.inbox, self.views, self.rs, self.ss = part, inbox, views, rs, ss

    def add(self, i, cond):
        def do():
            self.book.got(self.inbox(i), self.rs(i))
            for a, b in zip(self.views(self.part(i)), self.views(self.inbox(i))):
                add_rows(a, [a, b])

        pl.when(cond)(do)

    def step(self, t):
        r, last = self.at.r, self.groups - 1
        i = last - t + r
        go = jnp.logical_and(t >= r, r < last)
        self.add(i, jnp.logical_and(go, r > 0))
        self.book.send(self.part(i), self.inbox(i), self.ss(0, t), self.rs(i), self.at.up, go)
        m = last - r
        i = t - m
        go = jnp.logical_and(t >= m, r > 0)
        self.add(i, jnp.logical_and(go, r < last))
        to = jnp.where(i == r - 1, self.groups, i)
        self.book.send(self.part(i), self.inbox(to), self.ss(1, t), self.rs(to), self.at.dn, go)

    def final(self, outs):
        r, last = self.at.r, self.groups - 1
        up, dn = self.inbox(r), self.inbox(self.groups)

        def total(refs):
            for out, *terms in zip(outs, *[self.views(ref) for ref in refs]):
                add_rows(out, terms)

        self.book.got(up, self.rs(r), r > 0)
        self.book.got(dn, self.rs(self.groups), r < last)
        mine = self.part(r)
        pl.when(r == 0)(lambda: total([mine, dn]))
        pl.when(r == last)(lambda: total([mine, up]))
        pl.when(jnp.logical_and(r > 0, r < last))(lambda: total([mine, up, dn]))


def sum_kernel(
    R, parts, q_i, gc_i, o_i, gu_i, wd_i, y_i, q_o, o_o, gu_o, wd_o, y_o,
    qm, qc, qd, qx, qy, qs, om, oc, od, ox, oy, os_, qz, qzr, qzs, oz, ozr, ozs,
    gm, gz, gzr, gzs, dm, dz, dzr, dzs, gf, gas, gar, lsem,
    ym, yc, yd, yx, yy, ys,
):
    at = place()
    meet(at, R, "all", True)
    book = Book(at)
    r = at.r
    wide = q_i.shape[-1]

    def whole(ref):
        return [ref]

    def many(ref):
        return [ref.at[j] for j in range(GROUP)]

    gm_load = pltpu.make_async_copy(gu_i, gm, lsem.at[0])
    dm_load = pltpu.make_async_copy(wd_i, dm, lsem.at[1])
    gm_load.start()
    dm_load.start()

    order = []
    for i in range((R + 1) // 2):
        order += [R - 1 - i] + ([i] if i < R - 1 - i else [])
    items, outs = [], []
    for i in order:
        items.append(
            PlaneSum(
                at, book, i % 2 == 1, [(lambda c, i=i: o_i.at[i, :, c], lambda buf: buf)],
                om.at[i], oc.at[i], od.at[i], ox.at[i], oy.at[i], lambda j, i=i: os_.at[i, j],
            )
        )
        outs.append(om.at[i, at.k0])
    for i in order:
        items.append(
            PlaneSum(
                at, book, i % 2 == 1,
                [
                    (lambda c, i=i: q_i.at[i, :, c], lambda buf: buf.at[:, :, pl.ds(0, wide)]),
                    (lambda c, i=i: gc_i.at[i, :, c], lambda buf: buf.at[:, :, pl.ds(wide, 128)]),
                ],
                qm.at[i], qc.at[i], qd.at[i], qx.at[i], qy.at[i], lambda j, i=i: qs.at[i, j],
            )
        )
        outs.append(qm.at[i, at.k0])
    attn = len(items)
    items += row_items(at, book, y_i, parts, ym, yc, yd, yx, yy, ys)
    rows = y_o.shape[0] // parts
    outs += [y_o.at[pl.ds(i * rows, rows)] for i in range(parts)]

    gu_sum = LineSum(
        at, book, R, None, lambda i: gm.at[i], lambda i: gz.at[i], many,
        lambda i: gzr.at[i], lambda k, t: gzs.at[k, t],
    )
    wd_sum = LineSum(
        at, book, R, None, lambda i: dm.at[i], lambda i: dz.at[i], whole,
        lambda i: dzr.at[i], lambda k, t: dzs.at[k, t],
    )
    q_sum = LineSum(
        at, book, R, None, lambda i: qm.at[i, at.k0], lambda i: qz.at[i], whole,
        lambda i: qzr.at[i], lambda k, t: qzs.at[k, t],
    )
    o_sum = LineSum(
        at, book, R, None, lambda i: om.at[i, at.k0], lambda i: oz.at[i], whole,
        lambda i: ozr.at[i], lambda k, t: ozs.at[k, t],
    )

    for item in items[:attn]:
        item.start()
    dm_load.wait()
    gm_load.wait()

    own = pltpu.make_async_copy(gf.at[at.p], gu_o.at[at.p], lsem.at[2])

    def mlp_end():
        gu_sum.final(many(gf))
        own.start()
        for k in range(1, GROUP):
            t = lax.rem(at.p + k, GROUP)
            book.send(gf.at[t], gu_o.at[at.p], gas.at[k - 1], gar.at[k - 1], at.me - at.p + t)
        wd_sum.final(whole(wd_o))

    def mlp(t):
        gu_sum.step(t)
        wd_sum.step(t)

    def att(t):
        o_sum.step(t)
        q_sum.step(t)

    hooks = {}
    for t in range(R - 1):
        hooks.setdefault((t * attn) // (R - 1), []).append(functools.partial(mlp, t))
        hooks.setdefault(attn + 2 + (t * parts) // (R - 1), []).append(functools.partial(att, t))
    hooks.setdefault(attn + 2, []).append(mlp_end)

    total = len(items)
    for i in range(total + 2):
        for hook in hooks.get(i, ()):
            hook()
        if i == 2:
            for item in items[attn:]:
                item.start()
        if i < total:
            items[i].first()
        if 1 <= i <= total:
            items[i - 1].second()
        if i >= 2:
            items[i - 2].third(outs[i - 2])
    q_sum.final(whole(q_o))
    o_sum.final(whole(o_o))
    for k in range(1, GROUP):
        t = lax.rem(at.p + GROUP - k, GROUP)
        book.got(gu_o.at[t], gar.at[k - 1])
    own.wait()
    book.drain()


def sum_all(R, q, gc, o, gu, wd, y):
    rows, parts = q.shape[3], 4
    wide, mid, two = q.shape[4] + gc.shape[4], o.shape[4], gu.shape[3]
    deep, width = wd.shape[1:]
    steps = max(R - 1, 1)

    def attn(columns):
        return [
            pltpu.VMEM((R, 4, rows, columns), BF),
            pltpu.VMEM((R, 4, rows, columns), BF),
            pltpu.VMEM((R, rows, columns), BF),
            pltpu.VMEM((R, rows, columns), BF),
            pltpu.VMEM((R, rows, columns), BF),
            DMA((R, 12)),
        ]

    return pl.pallas_call(
        functools.partial(sum_kernel, R, parts),
        out_shape=(
            jax.ShapeDtypeStruct((rows, wide), F32),
            jax.ShapeDtypeStruct((rows, mid), F32),
            jax.ShapeDtypeStruct((GROUP, rows, two), BF),
            jax.ShapeDtypeStruct((deep, width), F32),
            jax.ShapeDtypeStruct(y.shape[2:], F32),
        ),
        in_specs=[ANY] * 6,
        out_specs=(VM, VM, ANY, VM, VM),
        scratch_shapes=attn(wide) + attn(mid) + [
            pltpu.VMEM((R + 1, rows, wide), BF), DMA((R + 1,)), DMA((2, steps)),
            pltpu.VMEM((R + 1, rows, mid), BF), DMA((R + 1,)), DMA((2, steps)),
            pltpu.VMEM((R, GROUP, rows, two), BF), pltpu.VMEM((R + 1, GROUP, rows, two), BF),
            DMA((R + 1,)), DMA((2, steps)),
            pltpu.VMEM((R, deep, width), BF), pltpu.VMEM((R + 1, deep, width), BF),
            DMA((R + 1,)), DMA((2, steps)),
            pltpu.VMEM((GROUP, rows, two), BF), DMA((7,)), DMA((7,)), DMA((3,)),
        ] + row_scratch(parts, *y.shape[2:]),
        compiler_params=pltpu.CompilerParams(
            collective_id=3, has_side_effects=True, vmem_limit_bytes=60 * 2**20
        ),
    )(q, gc, o, gu, wd, y)


def rotary_tables(length, width):
    half = width // 2
    position = jnp.arange(length, dtype=jnp.float32)
    inverse = THETA ** (-(jnp.arange(half, dtype=jnp.float32) * 2.0) / width)
    angles = position[:, None] * inverse[None, :]
    return (jnp.cos(angles)[:, None, :], jnp.sin(angles)[:, None, :])


def rotate(values, cosine, sine):
    half = values.shape[-1] // 2
    first = values[..., :half]
    second = values[..., half:]
    return jnp.concatenate(
        [first * cosine - second * sine, second * cosine + first * sine], axis=-1
    )


def rotate_back(grads, cosine, sine):
    half = grads.shape[-1] // 2
    first = grads[..., :half]
    second = grads[..., half:]
    return jnp.concatenate(
        [first * cosine + second * sine, second * cosine - first * sine], axis=-1
    )


def matmul(left, right):
    return jnp.dot(left, right, preferred_element_type=jnp.float32)


def rows_inner(left, right):
    return lax.dot_general(
        left, right, (((0,), (0,)), ((), ())), preferred_element_type=jnp.float32
    )


def times_transposed(left, right):
    return lax.dot_general(
        left, right, (((1,), (1,)), ((), ())), preferred_element_type=jnp.float32
    )


def rms_forward(values, gain):
    inverse = lax.rsqrt(jnp.mean(values * values, axis=-1, keepdims=True) + EPSILON)
    normed = values * inverse
    return (normed, inverse, (normed * gain).astype(jnp.bfloat16))


def rms_backward(grad_in, normed, inverse, gain):
    scaled = grad_in * gain
    gain_grad = jnp.sum(grad_in * normed, axis=0)
    input_grad = inverse * (scaled - normed * jnp.mean(scaled * normed, axis=-1, keepdims=True))
    return (input_grad, gain_grad)


def block_scores(query_rot, key_rot, scale):
    length = query_rot.shape[0]
    scores = (
        jnp.einsum("qkrd,tkd->krqt", query_rot, key_rot, preferred_element_type=jnp.float32) * scale
    )
    allowed = jnp.arange(length)[None, :] <= jnp.arange(length)[:, None]
    return jnp.where(allowed, scores, -1e30)


def pad_rows(array, axis, rows):
    pad = [(0, 0)] * array.ndim
    pad[axis] = (0, rows - array.shape[axis])
    return jnp.pad(array, pad) if rows != array.shape[axis] else array


def body(
    R, tokens, norm1_gain, w_query, w_key, w_value, w_out, norm2_gain, w_gate, w_up, w_down, cotangent
):
    length, width = tokens.shape
    n = R * GROUP
    own = w_query.shape[0]
    rows = -(-own // 16) * 16
    deep = w_down.shape[0]
    per_group = HEADS // KV_HEADS
    scale = HEAD_DIM ** (-0.5)
    cosine, sine = rotary_tables(length, HEAD_DIM)
    nq, nk = HEADS * HEAD_DIM, KV_HEADS * HEAD_DIM

    gains = jnp.concatenate([norm1_gain[:, None], norm2_gain[:, None]], axis=1)
    q_shard = pad_rows(
        jnp.concatenate([w_query, w_key, w_value, jnp.pad(gains, ((0, 0), (0, 126)))], axis=1), 0, rows
    )
    o_shard = pad_rows(w_out, 0, rows)

    def by_place(w):
        return w.reshape(own, R, GROUP, deep).transpose(2, 0, 1, 3).reshape(GROUP, own, R * deep)

    gu_shard = pad_rows(jnp.concatenate([by_place(w_gate), by_place(w_up)], axis=2), 1, rows)
    q_all, o_all, gu_all, wd_all, e_all = gather_weights(
        R, q_shard, o_shard, gu_shard, w_down, cotangent
    )

    def whole(a):
        return a[:, :own].reshape(n * own, a.shape[2])

    qkv_weight, out_weight, gu_weight = whole(q_all), whole(o_all), whole(gu_all)
    down_weight = wd_all.reshape(R * deep, width)
    gain_one = qkv_weight[:, nq + 2 * nk].astype(F32)
    gain_two = qkv_weight[:, nq + 2 * nk + 1].astype(F32)

    inputs = tokens.astype(jnp.float32)
    normed_one, inv_one, act_one = rms_forward(inputs, gain_one)
    raw = matmul(act_one, qkv_weight)
    query_raw = raw[:, :nq].reshape(length, HEADS, HEAD_DIM)
    key_raw = raw[:, nq : nq + nk].reshape(length, KV_HEADS, HEAD_DIM)
    value_low = raw[:, nq + nk : nq + 2 * nk].astype(BF).reshape(length, KV_HEADS, HEAD_DIM)
    query_rot = (
        rotate(query_raw, cosine, sine).astype(BF).reshape(length, KV_HEADS, per_group, HEAD_DIM)
    )
    key_rot = rotate(key_raw, cosine, sine).astype(BF)
    scores = block_scores(query_rot, key_rot, scale)
    peak = jnp.max(scores, axis=-1, keepdims=True)
    expo = jnp.exp(scores - peak)
    total = jnp.sum(expo, axis=-1, keepdims=True)
    probs = (expo / total).astype(BF)
    lse = peak + jnp.log(total)
    heads_out = jnp.einsum("krqt,tkd->qkrd", probs, value_low, preferred_element_type=F32)
    attended = heads_out.reshape(length, nq).astype(BF)
    mixed = inputs + matmul(attended, out_weight)
    normed_two, inv_two, act_two = rms_forward(mixed, gain_two)

    act_all = spread(act_two).reshape(GROUP * length, width)
    cot_all = e_all.reshape(GROUP * length, width)
    hid = R * deep
    pair = matmul(act_all, gu_weight)
    gate_val, up_val = pair[:, :hid], pair[:, hid:]
    sigma = jax.nn.sigmoid(gate_val)
    silu_val = gate_val * sigma
    hidden = (silu_val * up_val).astype(BF)
    out_part = matmul(hidden, down_weight).astype(BF)
    hidden_grad = times_transposed(cot_all, down_weight)
    gate_grad_b = (hidden_grad * up_val * sigma * (1.0 + gate_val * (1.0 - sigma))).astype(BF)
    up_grad_b = (hidden_grad * silu_val).astype(BF)
    pair_grad = jnp.concatenate([gate_grad_b, up_grad_b], axis=1)
    act_part = times_transposed(pair_grad, gu_weight).astype(BF)
    act_two_grad = fold(act_part.reshape(4, 2, length, width))
    gu_part = rows_inner(act_all, pair_grad).astype(BF)
    wd_part = rows_inner(hidden, cot_all).astype(BF)

    grad_out = cotangent.astype(jnp.float32)
    mixed_part, gain_two_grad = rms_backward(act_two_grad, normed_two, inv_two, gain_two)
    mixed_grad = grad_out + mixed_part

    branch_grad = mixed_grad.astype(BF)
    attended_grad = (
        times_transposed(branch_grad, out_weight)
        .astype(BF)
        .reshape(length, KV_HEADS, per_group, HEAD_DIM)
    )
    scores = block_scores(query_rot, key_rot, scale)
    probs = jnp.exp(scores - lse)
    probs_low = probs.astype(BF)
    prob_grad = jnp.einsum(
        "qkrd,tkd->krqt", attended_grad, value_low, preferred_element_type=jnp.float32
    )
    center = jnp.sum(probs * prob_grad, axis=-1, keepdims=True)
    score_grad = (probs * (prob_grad - center)).astype(BF)
    query_grads = (
        jnp.einsum("krqt,tkd->qkrd", score_grad, key_rot, preferred_element_type=jnp.float32)
        * scale
    )
    key_term = (
        jnp.einsum("krqt,qkrd->tkd", score_grad, query_rot, preferred_element_type=jnp.float32)
        * scale
    )
    value_term = jnp.einsum(
        "krqt,qkrd->tkd", probs_low, attended_grad, preferred_element_type=jnp.float32
    )
    query_raw_grad = (
        rotate_back(query_grads.reshape(length, HEADS, HEAD_DIM), cosine, sine)
        .astype(BF)
        .reshape(length, nq)
    )
    key_raw_grad = rotate_back(key_term, cosine, sine).astype(BF).reshape(length, nk)
    value_raw_grad = value_term.astype(BF).reshape(length, nk)
    raw_grad = jnp.concatenate([query_raw_grad, key_raw_grad, value_raw_grad], axis=1)
    qkv_part = rows_inner(act_one, raw_grad).astype(BF)
    raw_grad_wide = jnp.pad(raw_grad, ((0, 0), (0, 128)))
    act_one_grad = times_transposed(raw_grad_wide, qkv_weight)
    input_part, gain_one_grad = rms_backward(act_one_grad, normed_one, inv_one, gain_one)
    grad_tokens = mixed_grad + input_part
    o_part = rows_inner(attended, branch_grad).astype(BF)
    gain_part = jnp.pad(
        jnp.stack([gain_one_grad, gain_two_grad], axis=1), ((0, 0), (0, 126))
    ).astype(BF)

    def split(a):
        return pad_rows(a.reshape(R, 4, 2, own, a.shape[1]), 3, rows)

    q_sum, o_sum, gu_sum, wd_sum, out_sum = sum_all(
        R,
        split(qkv_part),
        split(gain_part),
        split(o_part),
        pad_rows(gu_part.reshape(R, GROUP, own, 2 * hid), 2, rows),
        wd_part.reshape(R, deep, width),
        out_part.reshape(4, 2, length, width),
    )
    output = (mixed + out_sum).astype(BF)

    def columns(a):
        a = a[:, :own].reshape(GROUP, own, R, deep).transpose(1, 2, 0, 3)
        return a.reshape(own, R * GROUP * deep).astype(F32)

    q_sum, o_sum = q_sum[:own], o_sum[:own]
    return (
        output,
        grad_tokens,
        q_sum[:, nq + 2 * nk],
        q_sum[:, :nq],
        q_sum[:, nq : nq + nk],
        q_sum[:, nq + nk : nq + 2 * nk],
        o_sum,
        q_sum[:, nq + 2 * nk + 1],
        columns(gu_sum[:, :, :hid]),
        columns(gu_sum[:, :, hid:]),
        wd_sum,
    )


def solution(mesh):
    n = mesh.shape[AXIS]
    in_specs = (
        P(AXIS, None),
        P(AXIS),
        P(AXIS, None),
        P(AXIS, None),
        P(AXIS, None),
        P(AXIS, None),
        P(AXIS),
        P(AXIS, None),
        P(AXIS, None),
        P(AXIS, None),
        P(AXIS, None),
    )
    out_specs = (
        P(AXIS, None),
        P(AXIS, None),
        P(AXIS),
        P(AXIS, None),
        P(AXIS, None),
        P(AXIS, None),
        P(AXIS, None),
        P(AXIS),
        P(AXIS, None),
        P(AXIS, None),
        P(AXIS, None),
    )
    return jax.shard_map(
        functools.partial(body, n // GROUP),
        mesh=mesh,
        in_specs=in_specs,
        out_specs=out_specs,
        check_vma=False,
    )
```

time: 1840 us -> 534 us (0.29)
  waiting for transfers between devices: 1540 us -> 0 us
  Pallas kernels: 0 us -> 390 us
  matrix products: 131 us -> 84.9 us
  blocking collectives: 42.2 us -> 0 us
  starting transfers between devices: 36.6 us -> 0 us
  other arithmetic: 53 us -> 20.1 us
    all_to_all x9 -> x0, waiting for transfers between devices: 1070 us -> none  [the longest x1 269 us: body(): lax.all_to_all(by_owner(up_grad, devices).astype(jnp.bfloat16), 'fsdp', s...]
    all_gather x7 -> x0, waiting for transfers between devices: 457 us -> none  [the longest x1 93.4 us: body(): lax.all_gather(w_up, 'fsdp', axis=0, tiled=True)]
    pallas_call x0 -> x4, Pallas kernels: none -> 390 us  [the longest x1 167 us: gather_weights(): pl.pallas_call(functools.partial(gather_kernel, R, parts), out_shape=(jax...]
    unnamed x1 -> x0, blocking collectives: 42.2 us -> none
    reduce_sum x9 -> x0, other arithmetic: 39.9 us -> none  [owner_totals(): return tuple((jnp.sum(piece, axis=0) for piece in received))]
    all_to_all x9 -> x0, starting transfers between devices: 36.4 us -> none  [the longest x1 5.89 us: body(): lax.all_to_all(by_owner(gain_one_grad, devices).astype(jnp.bfloat16), 'fs...]
    dot_general x7 -> x4, matrix products: 45.8 us -> 26 us  [rows_inner(): lax.dot_general(left, right, (((0,), (0,)), ((), ())), preferred_element_...]
    dot_general x7 -> x4, matrix products: 40.3 us -> 26.3 us  [matmul(): return jnp.dot(left, right, preferred_element_type=jnp.float32)]
  transfers between devices with their start and end apart: 16 -> 0, of which waited for: 15 -> 0; matrix products, arithmetic and copies ran while one was open for 8% -> 0% of each run, Pallas kernels for 0% -> 0%
where the time goes in v1:
time: 534 us; the launch traced here: 526 us
  Pallas kernels  390 us (73%)
  matrix products  84.9 us (16%)
  local copies, waits for them, and re-layouts  29.1 us (5%)
  other arithmetic  20.1 us (4%)
    pallas_call x1, Pallas kernels, gather_weights(): pl.pallas_call(functools.partial(gather_kernel, R, parts), out_shape=(jax...  167 us
    pallas_call x1, Pallas kernels, sum_all(): pl.pallas_call(functools.partial(sum_kernel, R, parts), out_shape=(jax.Sh...  142 us
    pallas_call x1, Pallas kernels, spread(): pl.pallas_call(functools.partial(spread_kernel, parts), out_shape=jax.Sha...  43.9 us
    pallas_call x1, Pallas kernels, fold(): pl.pallas_call(functools.partial(fold_kernel, parts), out_shape=jax.Shape...  37.2 us
    dot_general x4, matrix products, matmul(): return jnp.dot(left, right, preferred_element_type=jnp.float32)  26.3 us
    dot_general x4, matrix products, rows_inner(): lax.dot_general(left, right, (((0,), (0,)), ((), ())), preferred_element_...  26 us
    dot_general x4, matrix products, times_transposed(): lax.dot_general(left, right, (((1,), (1,)), ((), ())), preferred_element_...  24.3 us
    unnamed x113, local copies, waits for them, and re-layouts  11.4 us

profile of v1, /device:TPU:0, one launch (start us, length us, event | category | flops | bytes accessed | tf_op | source)
XLA Modules:
  0.0 526.2 jit_solution(16184134962560158439)
XLA Ops:
  8.9 167.2 %shard_map.194 = (bf16[32,48,3200]{2,1,0:T(8,128)(2,1)}, bf16[32,48,1536]{2,1,0:T(8,128)(2,1)}, bf16[32,48,1024]{2,1,0:T(8,128)(2,1)}, bf16[4,128,1536]{2,1,0:T(8,128)(2,1)}, bf16[8,256,1536]{2,1,0:T(8,128)(2,1)}) custom-call(bf16[48,3200]{1,0:T(8,128)(2,1)} %fusion.35.q_i, bf16[48,1536]{1,0:T(8,128)(2,1)} %o_i.1, ...), custom_call_target="tpu_custom_call" | custom-call | tf_op jit(solution)/shard_map/pallas_call | solution.py:290
  178.5 6.7 %fusion.37 = f32[256,3200]{1,0:T(8,128)S(1)} fusion(bf16[1536,3200]{1,0:T(8,128)(2,1)} %bitcast.168, bf16[256,1536]{1,0:T(8,128)(2,1)S(1)} %copy-done.2, f32[1536]{0:T(1024)S(1)} %convert_reduce_fusion.1, f32[256]{0:T(256)S(1)} %add_rsqrt_fusion.1), kind=kOutput, calls=%fused_computation.83 | convolution fusion | flops 2518155264 | bytes 13900800 | tf_op jit(solution)/shard_map/dot_general | solution.py:704
  187.2 2.7 slice.94
  189.9 1.9 copy.69
  191.8 1.9 subtract_convert_fusion.1
  195.0 1.8 fusion.49
  203.4 43.9 %shard_map.195 = bf16[8,256,1536]{2,1,0:T(8,128)(2,1)} custom-call(bf16[256,1536]{1,0:T(8,128)(2,1)} %multiply_convert_fusion.3.a_i), custom_call_target="tpu_custom_call" | custom-call | tf_op jit(solution)/shard_map/pallas_call | solution.py:328
  247.3 12.6 %fusion.50 = f32[2048,1024]{0,1:T(8,128)} fusion(bf16[2048,1536]{1,0:T(8,128)(2,1)} %bitcast.130, bf16[1536,1024]{1,0:T(8,128)(2,1)} %bitcast.176), kind=kOutput, calls=%fused_computation.108 | convolution fusion | flops 6442450944 | bytes 17825792 | tf_op jit(solution)/shard_map/dot_general | solution.py:704
  259.9 9.0 %multiply_convert_fusion.2 = (bf16[2048,512]{0,1:T(8,128)(2,1)S(1)}, bf16[2048,512]{0,1:T(8,128)(2,1)S(1)}, bf16[2048,512]{0,1:T(8,128)(2,1)S(1)}) fusion(f32[2048,1024]{0,1:T(8,128)} %fusion.50, bf16[2048,1536]{1,0:T(8,128)(2,1)} %bitcast.172, bf16[512,1536]{1,0:T(8,128)(2,1)S(1)} %bitcast.178), kind=kOutput, calls=%fused_computation.13 | convolution fusion | flops 3236954112 | bytes 22544384 | tf_op jit(solution)/shard_map/dot_general | solution.py:714
  268.9 4.6 convolution_convert_fusion.5
  273.5 9.1 %convolution_convert_fusion.4 = bf16[1536,1024]{1,0:T(8,128)(2,1)} fusion(bf16[2048,1536]{1,0:T(8,128)(2,1)S(1)} %bitcast.133, bf16[2048,512]{0,1:T(8,128)(2,1)S(1)} %get-tuple-element.38, bf16[2048,512]{0,1:T(8,128)(2,1)S(1)} %get-tuple-element.37), kind=kOutput, calls=%fused_computation.19 | convolution fusion | flops 6452412416 | bytes 13631488 | tf_op jit(solution)/shard_map/dot_general | solution.py:708
  282.7 8.9 %convolution_convert_fusion.3 = bf16[2048,1536]{1,0:T(8,128)(2,1)} fusion(bf16[1536,1024]{1,0:T(8,128)(2,1)S(1)} %bitcast.177, bf16[2048,512]{0,1:T(8,128)(2,1)S(1)} %get-tuple-element.38, bf16[2048,512]{0,1:T(8,128)(2,1)S(1)} %get-tuple-element.37), kind=kOutput, calls=%fused_computation.3 | convolution fusion | flops 6453985280 | bytes 13631488 | tf_op jit(solution)/shard_map/dot_general | solution.py:714
  291.6 37.2 %shard_map.196 = f32[256,1536]{1,0:T(8,128)S(1)} custom-call(bf16[4,2,256,1536]{3,2,1,0:T(8,128)(2,1)} %bitcast.137), custom_call_target="tpu_custom_call" | custom-call | tf_op jit(solution)/shard_map/pallas_call | solution.py:461
  331.0 2.3 convolution_convert_fusion.6
  333.3 2.3 copy.72
  336.3 3.4 fusion.29
  346.6 4.2 fusion.18
  352.3 1.8 pad.15.clone
  354.1 4.8 convolution_convert_fusion.2
  358.9 5.6 %convolution_convert_fusion.1 = bf16[2048,1536]{1,0:T(8,128)(2,1)} fusion(bf16[2048,512]{0,1:T(8,128)(2,1)S(1)} %copy-done.41, bf16[512,1536]{1,0:T(8,128)(2,1)S(1)} %bitcast.179), kind=kOutput, calls=%fused_computation.1 | convolution fusion | flops 3224371200 | bytes 9961472 | tf_op jit(solution)/shard_map/dot_general | solution.py:704
  364.5 7.5 %convolution_convert_fusion = bf16[1536,3072]{1,0:T(8,128)(2,1)} fusion(bf16[256,1536]{1,0:T(8,128)(2,1)S(1)} %copy-done.4, f32[1536]{0:T(1024)S(1)} %copy-done.31, f32[256]{0:T(256)S(1)} %copy-done.35, bf16[256,768]{0,1:T(8,128)(2,1)S(1)} %bitcast.141, bf16[256,768]{0,1:T(8,128)(2,1)S(1)} %bitcast.139, bf16[256,1536]{0,1:T(8,128)(2,1)S(1)} %bitcast.127), kind=kOutput, calls=%fused_computation | convolution fusion | flops 2426929152 | bytes 11803648 | tf_op jit(solution)/shard_map/dot_general | solution.py:708
  371.9 142.1 %shard_map.197 = (f32[48,3200]{1,0:T(8,128)}, f32[48,1536]{1,0:T(8,128)}, bf16[8,48,1024]{2,1,0:T(8,128)(2,1)}, f32[128,1536]{1,0:T(8,128)}, f32[256,1536]{1,0:T(8,128)}) custom-call(bf16[4,4,2,48,3072]{4,3,2,1,0:T(8,128)(2,1)} %bitcast.116, bf16[4,4,2,48,128]{4,3,2,1,0:T(8,128)(2,1)} %bitcast.159, bf16[4,4,2,48,1536]{4,3,2,1,0:T(8,128)(2,1)} %bitcast.117, ...), custom_call_target="tpu_custom_call" | custom-call | tf_op jit(solution)/shard_map/pallas_call | solution.py:651
  514.1 4.0 fusion.21
  522.1 2.2 copy_bitcast_fusion
  (170 shorter events, 36.9 us)
Async XLA Ops:
  0.6 6.9 %copy-start.26 = (bf16[48,4096]{1,0:T(8,128)(2,1)S(1)}, bf16[48,4096]{1,0:T(8,128)(2,1)}, u32[]{:S(2)}) copy-start(bf16[48,4096]{1,0:T(8,128)(2,1)} %param.19) | copy-start | bytes 1179652
  2.8 175.7 %copy-start.33 = (f32[256]{0:T(256)}, f32[256]{0:T(256)S(1)}, u32[]{:S(2)}) copy-start(f32[256]{0:T(256)S(1)} %add_rsqrt_fusion.1) | copy-start | bytes 3076
  8.9 169.5 %copy-start.2 = (bf16[256,1536]{1,0:T(8,128)(2,1)S(1)}, bf16[256,1536]{1,0:T(8,128)(2,1)}, u32[]{:S(2)}) copy-start(bf16[256,1536]{1,0:T(8,128)(2,1)} %param.11) | copy-start | bytes 2359300
  178.5 6.7 %copy-start.30 = (f32[1536]{0:T(1024)}, f32[1536]{0:T(1024)S(1)}, u32[]{:S(2)}) copy-start(f32[1536]{0:T(1024)S(1)} %convert_reduce_fusion.1) | copy-start | bytes 18436
  202.3 126.5 %copy-start.32 = (f32[256]{0:T(256)}, f32[256]{0:T(256)S(1)}, u32[]{:S(2)}) copy-start(f32[256]{0:T(256)S(1)} %add_rsqrt_fusion) | copy-start | bytes 3076
  247.3 12.6 %copy-start.38 = (bf16[4,128,1536]{2,1,0:T(8,128)(2,1)S(1)}, bf16[4,128,1536]{2,1,0:T(8,128)(2,1)}, u32[]{:S(2)}) copy-start(bf16[4,128,1536]{2,1,0:T(8,128)(2,1)} %get-tuple-element.24) | copy-start | bytes 4718596
  247.3 21.6 %slice-start.10 = ((s8[6291456]{0:T(1024)(128)(4,1)}), s8[4194304]{0:T(1024)(128)(4,1)S(1)}, s32[]{:S(2)}) async-start(s8[6291456]{0:T(1024)(128)(4,1)} %bitcast.173), calls=%async_computation.10 | async-start | bytes 8388608
  247.3 26.2 %slice-start.4 = ((s8[6291456]{0:T(1024)(128)(4,1)}), s8[2097152]{0:T(1024)(128)(4,1)S(1)}, s32[]{:S(2)}) async-start(s8[6291456]{0:T(1024)(128)(4,1)} %bitcast.131), calls=%async_computation.4 | async-start | bytes 4194304
  259.9 9.0 %slice-start.11 = ((s8[6291456]{0:T(1024)(128)(4,1)}), s8[2097152]{0:T(1024)(128)(4,1)S(1)}, s32[]{:S(2)}) async-start(s8[6291456]{0:T(1024)(128)(4,1)} %bitcast.173), calls=%async_computation.11 | async-start | bytes 4194304
  259.9 13.6 %slice-start.5 = ((s8[6291456]{0:T(1024)(128)(4,1)}), s8[4194304]{0:T(1024)(128)(4,1)S(1)}, s32[]{:S(2)}) async-start(s8[6291456]{0:T(1024)(128)(4,1)} %bitcast.131), calls=%async_computation.5 | async-start | bytes 8388608
  268.9 4.6 copy-start.40
  273.5 9.2 %copy-start.37 = (bf16[32,48,1024]{2,1,0:T(8,128)(2,1)S(1)}, bf16[32,48,1024]{2,1,0:T(8,128)(2,1)}, u32[]{:S(2)}) copy-start(bf16[32,48,1024]{2,1,0:T(8,128)(2,1)} %get-tuple-element.25) | copy-start | bytes 9437188
  291.6 39.4 %slice-start.2 = ((s8[4718592]{0:T(1024)(128)(4,1)}), s8[4194304]{0:T(1024)(128)(4,1)S(1)}, s32[]{:S(2)}) async-start(s8[4718592]{0:T(1024)(128)(4,1)} %bitcast.121), calls=%async_computation.2 | async-start | bytes 8388608
  339.6 5.6 %copy-start.9 = (bf16[8,96,256]{2,1,0:T(8,128)(2,1)}, bf16[8,96,256]{2,1,0:T(8,128)(2,1)S(1)}, u32[]{:S(2)}) copy-start(bf16[8,96,256]{2,1,0:T(8,128)(2,1)S(1)} %fusion.29) | copy-start | bytes 1179652
  340.1 5.2 slice-start.7
  345.2 5.5 %copy-start.6 = (bf16[256,16,96]{0,2,1:T(8,128)(2,1)}, bf16[256,16,96]{0,2,1:T(8,128)(2,1)S(1)}, u32[]{:S(2)}) copy-start(bf16[256,16,96]{0,2,1:T(8,128)(2,1)S(1)} %pad_maximum_fusion.6) | copy-start | bytes 2359300
  354.1 4.8 copy-start.39
  354.1 4.8 copy-start.41
  358.9 5.6 %copy-start.4 = (bf16[256,1536]{1,0:T(8,128)(2,1)S(1)}, bf16[256,1536]{1,0:T(8,128)(2,1)}, u32[]{:S(2)}) copy-start(bf16[256,1536]{1,0:T(8,128)(2,1)} %param.11) | copy-start | bytes 2359300
  358.9 5.6 %copy-start.7 = (bf16[256,16,96]{0,2,1:T(8,128)(2,1)S(1)}, bf16[256,16,96]{0,2,1:T(8,128)(2,1)}, u32[]{:S(2)}) copy-start(bf16[256,16,96]{0,2,1:T(8,128)(2,1)} %copy-done.6) | copy-start | bytes 2359300
  358.9 5.6 %copy-start.10 = (bf16[8,96,256]{2,1,0:T(8,128)(2,1)S(1)}, bf16[8,96,256]{2,1,0:T(8,128)(2,1)}, u32[]{:S(2)}) copy-start(bf16[8,96,256]{2,1,0:T(8,128)(2,1)} %copy-done.9) | copy-start | bytes 1179652
  358.9 5.6 %copy-start.35 = (f32[256]{0:T(256)S(1)}, f32[256]{0:T(256)}, u32[]{:S(2)}) copy-start(f32[256]{0:T(256)} %copy-done.33) | copy-start | bytes 3076
  371.9 142.2 %copy-start.36 = (f32[256]{0:T(256)S(1)}, f32[256]{0:T(256)}, u32[]{:S(2)}) copy-start(f32[256]{0:T(256)} %broadcast_multiply_fusion) | copy-start | bytes 3076
  514.1 6.2 %copy-start.24 = (bf16[8,48,1024]{2,1,0:T(8,128)(2,1)S(1)}, bf16[8,48,1024]{2,1,0:T(8,128)(2,1)}, u32[]{:S(2)}) copy-start(bf16[8,48,1024]{2,1,0:T(8,128)(2,1)} %get-tuple-element.29) | copy-start | bytes 2359300
  (30 other events, 61.9 us)
